TPU v7x, 32 devices: a whole 2x2x4 slice. The times are simulated.
32 devices in a mesh: groups: 2 (over y), seq: 8 (over z, x), head: 2 (over core).
Axes of the slice: x: 2, y: 2, z: 4, core: 2. Of those that a mesh axis runs over, the one named last changes fastest.
Arguments:
- text_query_rows: bfloat16 [2048, 8192], P(('groups', 'seq'), 'head'), parts along dimension 0, may hold values from -40 to 40, as said below
- text_key_value: bfloat16 [2, 2048, 1024], P(None, ('groups', 'seq'), 'head'), parts along dimension 1, may hold values from -4 to 4, as said below
- doc_ids: int32 [2048], P(('groups', 'seq')), parts along dimension 0, may hold values from 0 to 3, never falling along the last dimension, each value on 1 to 512 neighbouring positions
- tile_span: int32 [2048, 2], P(('groups', 'seq')), parts along dimension 0, may hold values from 0 to 8, as said below
- vision_hidden: bfloat16 [4096, 1280], P(('groups', 'seq')), parts along dimension 0, may hold values from -6 to 6
- vision_qkv: bfloat16 [3, 4096, 1280], P(None, ('groups', 'seq'), 'head'), parts along dimension 1, may hold values from -6 to 6, as said below
- vision_out_weight: bfloat16 [1280, 1280], P('head'), may hold values from -0.625 to 0.625
- cross_keyvalue_weight: bfloat16 [1280, 2, 1024], P('seq', None, 'head'), may hold values from -0.15625 to 0.15625
- cross_gate: float32 [64], P('head'), may hold values from -1.5 to 1.5
Outputs:
- attention_out: bfloat16 [2048, 8192], P(('groups', 'seq'), 'head'), parts along dimension 0
There are 2 independent parts, one for each index of `groups`. A program takes and returns all parts, laid end to end along the dimension named above; an argument that names none is the same for every part. Nothing has to cross between parts.
Inputs may be any that keep to these rules, and one draw needn't show every extreme that they name: `tile_span`: each text token's span is an interval of the tiles of its own block b = p // 128 and of block b - 1 (first <= second, both between b - 1 and b + 1, never below 0); it may be empty. `doc_ids`: never falling along the document; each segment holds 1 to 512 tokens. `text_query_rows`: real values. `text_key_value`: real values. `vision_qkv`: real values.
All inputs are finite; a program needn't handle non-finite values.
Results may differ from a plain program's by a relative error of at most 0.024.
Values may be sent and summed in bfloat16 or wider, within the bound.
A program may use at most 64 MiB of HBM per device.

v0:
```python
import math

import jax
import jax.numpy as jnp
from jax import lax
from jax.sharding import PartitionSpec as P

HEAD_SIZE = 128
VHD = 80
WINDOW_BLOCKS = 2


def passed_along(block, axis, distance):
    devices = range(lax.axis_size(axis))
    route = [(i - distance, i) for i in devices if i - distance in devices]
    return lax.ppermute(block, axis, route)


def attend_heads(query_rows, keys, allowed_mask):
    scores = jnp.einsum(
        "tgrd,kgd->grtk", query_rows, keys, preferred_element_type=jnp.float32
    ) / math.sqrt(HEAD_SIZE)
    scores = jnp.where(allowed_mask[None, None], scores, -1e30)
    return jax.nn.softmax(scores, axis=-1)


def per_device(
    text_query_rows,
    text_key_value,
    doc_ids,
    tile_span,
    vision_hidden,
    vision_qkv,
    vision_out_weight,
    cross_keyvalue_weight,
    cross_gate,
):
    text_rows = text_query_rows.shape[0]
    tile_rows = vision_hidden.shape[0]
    kv_cols = text_key_value.shape[2]
    kv_heads = kv_cols // HEAD_SIZE
    query_group_ratio = text_query_rows.shape[1] // HEAD_SIZE // kv_heads
    seq_index = lax.axis_index("seq")
    vision_query = vision_qkv[0].reshape(tile_rows, -1, VHD)
    vision_key = vision_qkv[1].reshape(tile_rows, -1, VHD)
    vision_value = vision_qkv[2].reshape(tile_rows, -1, VHD)
    vision_scores = jnp.einsum(
        "qhd,khd->hqk", vision_query, vision_key, preferred_element_type=jnp.float32
    ) / math.sqrt(VHD)
    vision_weights = jax.nn.softmax(vision_scores, axis=-1).astype(jnp.bfloat16)
    vision_attn = jnp.einsum(
        "hqk,khd->qhd", vision_weights, vision_value, preferred_element_type=jnp.float32
    )
    vision_attn = vision_attn.astype(jnp.bfloat16).reshape(tile_rows, -1)
    partial_mix = jnp.dot(vision_attn, vision_out_weight, preferred_element_type=jnp.float32)
    mixed_sum = lax.psum(partial_mix, "head") + vision_hidden.astype(jnp.float32)
    image_norm = (
        mixed_sum * lax.rsqrt(jnp.mean(mixed_sum * mixed_sum, axis=-1, keepdims=True) + 1e-05)
    ).astype(jnp.bfloat16)
    image_key_value = jnp.einsum(
        "ic,cjf->ijf",
        image_norm,
        lax.all_gather(cross_keyvalue_weight, "seq", axis=0, tiled=True),
        preferred_element_type=jnp.float32,
    ).astype(jnp.bfloat16)
    earlier_tile = passed_along(image_key_value, "seq", 1)
    blocks = [(text_key_value, doc_ids)]
    current_kv, current_docs = (text_key_value, doc_ids)
    for repeat_count in range(WINDOW_BLOCKS):
        current_kv, current_docs = passed_along((current_kv, current_docs), "seq", 1)
        blocks.insert(0, (current_kv, current_docs))
    all_keyval = jnp.concatenate([member[0] for member in blocks], axis=1)
    all_docs = jnp.concatenate([member[1] for member in blocks], axis=0)
    key_pos = (seq_index - WINDOW_BLOCKS) * text_rows + jnp.arange(
        (WINDOW_BLOCKS + 1) * text_rows, dtype=jnp.int32
    )
    query_pos = seq_index * text_rows + jnp.arange(text_rows, dtype=jnp.int32)
    allowed_mask = (
        (all_docs[None, :] == doc_ids[:, None])
        & (key_pos[None, :] <= query_pos[:, None])
        & (key_pos[None, :] >= 0)
    )
    query_rows = text_query_rows.reshape(text_rows, kv_heads, query_group_ratio, HEAD_SIZE)
    self_attention_weights = attend_heads(
        query_rows, all_keyval[0].reshape(-1, kv_heads, HEAD_SIZE), allowed_mask
    ).astype(jnp.bfloat16)
    self_output = jnp.einsum(
        "ycmq,qyb->mycb",
        self_attention_weights,
        all_keyval[1].reshape(-1, kv_heads, HEAD_SIZE),
        preferred_element_type=jnp.float32,
    )
    self_output = self_output.reshape(text_rows, -1)
    image_all = jnp.concatenate([earlier_tile, image_key_value], axis=0)
    tile_ids = seq_index - 1 + jnp.arange(2 * tile_rows, dtype=jnp.int32) // tile_rows
    low_tile = tile_span[:, 0]
    high_tile = tile_span[:, 1]
    visible_mask = (tile_ids[None, :] >= low_tile[:, None]) & (
        tile_ids[None, :] < high_tile[:, None]
    )
    image_present = (high_tile > low_tile).astype(jnp.float32)
    cross_probabilities = (
        attend_heads(query_rows, image_all[:, 0].reshape(-1, kv_heads, HEAD_SIZE), visible_mask)
        * image_present[None, None, :, None]
    )
    cross_probabilities = cross_probabilities.astype(jnp.bfloat16)
    cross_output = jnp.einsum(
        "ycmq,qyb->mycb",
        cross_probabilities,
        image_all[:, 1].reshape(-1, kv_heads, HEAD_SIZE),
        preferred_element_type=jnp.float32,
    )
    cross_output = cross_output.reshape(text_rows, -1)
    gate_cols = jnp.repeat(jnp.tanh(cross_gate), HEAD_SIZE)
    return (self_output + gate_cols[None, :] * cross_output).astype(jnp.bfloat16)


def solution(mesh):
    placed = (
        P(("groups", "seq"), "head"),
        P(None, ("groups", "seq"), "head"),
        P(("groups", "seq")),
        P(("groups", "seq"), None),
        P(("groups", "seq"), None),
        P(None, ("groups", "seq"), "head"),
        P("head", None),
        P("seq", None, "head"),
        P("head"),
    )
    return jax.shard_map(
        per_device,
        mesh=mesh,
        in_specs=placed,
        out_specs=P(("groups", "seq"), "head"),
        check_vma=False,
    )
```

profile of v0, /device:TPU:24, one launch (start us, length us, event | category | flops | bytes accessed | tf_op | source)
XLA Modules:
  0.0 129.9 jit_solution(16018390959418832903)
XLA Ops:
  7.4 1.4 %fusion.35 = (bf16[1,256,640]{2,1,0:T(8,128)(2,1)S(1)}, bf16[1,256,640]{2,1,0:T(8,128)(2,1)S(1)}, bf16[1,256,640]{2,1,0:T(8,128)(2,1)S(1)}) fusion(bf16[3,256,640]{2,1,0:T(8,128)(2,1)} %param.14), kind=kLoop, calls=%fused_computation.67 | loop fusion | bytes 1966080 | tf_op jit(solution)/shard_map/slice | solution.py:45
  9.3 2.2 %fusion.38 = (f32[8,256]{1,0:T(8,128)S(1)}, f32[8,256,256]{1,2,0:T(8,128)}) fusion(bf16[256,8,80]{0,2,1:T(8,128)(2,1)S(1)} %bitcast.88, bf16[256,8,80]{0,2,1:T(8,128)(2,1)S(1)} %bitcast.87), kind=kOutput, calls=%fused_computation.70 | convolution fusion | flops 85459200 | bytes 2760704 | tf_op jit(solution)/shard_map/sub | solution.py:50
  11.5 1.9 %convolution_convert_fusion.1 = bf16[8,256,80]{1,2,0:T(8,128)(2,1)S(1)} fusion(bf16[256,8,80]{0,2,1:T(8,128)(2,1)S(1)} %bitcast.89, f32[8,256,256]{1,2,0:T(8,128)} %get-tuple-element.17, f32[8,256]{1,0:T(8,128)S(1)} %get-tuple-element.16), kind=kOutput, calls=%fused_computation.28 | convolution fusion | flops 85098496 | bytes 2760704 | tf_op jit(solution)/shard_map/hqk,khd->qhd/dot_general | solution.py:51
  13.5 1.8 %fusion.40 = f32[256,1280]{1,0:T(8,128)} fusion(bf16[256,640]{0,1:T(8,128)(2,1)S(1)} %bitcast.86, bf16[640,1280]{1,0:T(8,128)(2,1)S(1)} %copy-done), kind=kOutput, calls=%fused_computation.72 | convolution fusion | flops 419430400 | bytes 3276800 | tf_op jit(solution)/shard_map/dot_general | solution.py:55
  15.3 0.8 copy.33
  16.1 3.4 %collective-permute-start.2 = (s32[128]{0:T(128)S(1)}, s32[128]{0:T(128)S(1)}, u32[]{:S(2)}, u32[]{:S(2)}) collective-permute-start(s32[128]{0:T(128)S(1)} %copy-done.5), channel_id=1, source_target_pairs={{0,2},{2,4},{4,6},{6,8},{8,10},{10,12},{12,14},{1,3},{3,5},{5,7},{... | collective-permute-start | bytes 1544 | tf_op jit(solution)/shard_map/ppermute | solution.py:16
  19.7 1.9 %collective-permute-start = (bf16[2,128,512]{1,2,0:T(8,128)(2,1)S(1)}, bf16[2,128,512]{1,2,0:T(8,128)(2,1)S(1)}, u32[]{:S(2)}, u32[]{:S(2)}) collective-permute-start(bf16[2,128,512]{1,2,0:T(8,128)(2,1)S(1)} %copy.24), channel_id=1, source_target_pairs={{0,2},{2,4},{4,6},{6,8},{8,10},{10,12},{12,14},{1,3},{3,5},{5,7},{... | collective-permute-start | bytes 786440 | tf_op jit(solution)/shard_map/ppermute | solution.py:16
  21.9 0.5 collective-permute-done.2
  22.4 2.5 %collective-permute-start.3 = (s32[128]{0:T(128)S(1)}, s32[128]{0:T(128)S(1)}, u32[]{:S(2)}, u32[]{:S(2)}) collective-permute-start(s32[128]{0:T(128)S(1)} %collective-permute-done.2), channel_id=1, source_target_pairs={{0,2},{2,4},{4,6},{6,8},{8,10},{10,12},{12,14},{1,3},{3,5},{5,7},{... | collective-permute-start | bytes 1544 | tf_op jit(solution)/shard_map/ppermute | solution.py:16
  24.9 1.5 %copy.52 = bf16[16,8,32,128]{3,2,1,0:T(8,128)(2,1)S(1)} copy(bf16[16,8,32,128]{3,1,2,0:T(8,128)(2,1)} %bitcast.83) | data formatting | bytes 2097152
  26.4 5.7 %collective-permute-done = bf16[2,128,512]{1,2,0:T(8,128)(2,1)S(1)} collective-permute-done((bf16[2,128,512]{1,2,0:T(8,128)(2,1)S(1)}, bf16[2,128,512]{1,2,0:T(8,128)(2,1)S(1)}, u32[]{:S(2)}, u32[]{:S(2)}) %collective-permute-start) | collective-permute-done | bytes 262176 | tf_op jit(solution)/shard_map/ppermute | solution.py:16
  32.1 1.9 %collective-permute-start.1 = (bf16[2,128,512]{1,2,0:T(8,128)(2,1)S(1)}, bf16[2,128,512]{1,2,0:T(8,128)(2,1)S(1)}, u32[]{:S(2)}, u32[]{:S(2)}) collective-permute-start(bf16[2,128,512]{1,2,0:T(8,128)(2,1)S(1)} %collective-permute-done), channel_id=1, source_target_pairs={{0,2},{2,4},{4,6},{6,8},{8,10},{10,12},{12,14},{1,3},{3,5},{5,7},{... | collective-permute-start | bytes 786440 | tf_op jit(solution)/shard_map/ppermute | solution.py:16
  34.1 0.2 and_and_fusion
  34.3 12.1 %collective-permute-done.1 = bf16[2,128,512]{1,2,0:T(8,128)(2,1)S(1)} collective-permute-done((bf16[2,128,512]{1,2,0:T(8,128)(2,1)S(1)}, bf16[2,128,512]{1,2,0:T(8,128)(2,1)S(1)}, u32[]{:S(2)}, u32[]{:S(2)}) %collective-permute-start.1) | collective-permute-done | bytes 262176 | tf_op jit(solution)/shard_map/ppermute | solution.py:16
  46.5 0.8 fusion.36
  47.4 1.0 fusion.17
  48.4 3.7 %fusion.37 = (f32[4,8,128]{2,1,0:T(8,128)S(1)}, f32[4,8,128,384]{2,3,1,0:T(8,128)}) fusion(f32[4,384,128,8]{2,1,3,0:T(8,128)S(1)} %fusion.17, pred[128,384]{0,1:T(8,128)(4,1)S(1)} %and_and_fusion), kind=kOutput, calls=%fused_computation.69 | output fusion | flops 9437567 | bytes 12648448 | tf_op jit(solution)/shard_map/sub | solution.py:24
  52.1 1.6 %multiply_reduce_fusion.1 = f32[256]{0:T(256)S(1)} fusion(f32[256,1280]{1,0:T(8,128)} %all-reduce.2.cloned.1.call-done, bf16[256,1280]{1,0:T(8,128)(2,1)S(1)} %copy-done.1), kind=kLoop, calls=%fused_computation.25 | loop fusion | flops 1310464 | bytes 1967104 | tf_op jit(solution)/shard_map/reduce_sum | solution.py:58
  53.7 21.8 %all-gather.2.cloned.1.call-done = bf16[1280,2,512]{2,0,1:T(8,128)(2,1)} async-done(((bf16[160,2,512]{2,0,1:T(8,128)(2,1)}), bf16[1280,2,512]{2,0,1:T(8,128)(2,1)}) %all-gather.2.cloned.1.call-update) | async-done | bytes 2621456 | tf_op jit(solution)/shard_map/all_gather | solution.py:63
  75.5 3.9 %convolution_convert_fusion = bf16[256,2,512]{2,0,1:T(8,128)(2,1)} fusion(bf16[1280,2,512]{2,0,1:T(8,128)(2,1)} %all-gather.2.cloned.1.call-done, f32[256,1280]{1,0:T(8,128)} %all-reduce.2.cloned.1.call-done, bf16[256,1280]{1,0:T(8,128)(2,1)S(1)} %copy-done.1, f32[256]{0:T(256)S(1)} %add_rsqrt_fusion), kind=kOutput, calls=%fused_computation.27 | convolution fusion | flops 672661504 | bytes 5112832 | tf_op jit(solution)/shard_map/ic,cjf->ijf/dot_general | solution.py:60
  79.4 2.6 %collective-permute-start.4 = (bf16[256,2,512]{2,0,1:T(8,128)(2,1)}, bf16[256,2,512]{2,0,1:T(8,128)(2,1)S(1)}, u32[]{:S(2)}, u32[]{:S(2)}) collective-permute-start(bf16[256,2,512]{2,0,1:T(8,128)(2,1)} %convolution_convert_fusion), channel_id=1, source_target_pairs={{0,2},{2,4},{4,6},{6,8},{8,10},{10,12},{12,14},{1,3},{3,5},{5,7},{... | collective-permute-start | bytes 1572872 | tf_op jit(solution)/shard_map/ppermute | solution.py:16
  82.0 4.9 %fusion.11 = f32[4,128,8,128]{3,1,2,0:T(8,128)} fusion(bf16[384,4,128,1]{0,2,3,1:T(8,128)(2,1)S(1)} %bitcast.85, f32[4,8,128,384]{2,3,1,0:T(8,128)} %get-tuple-element.15, f32[4,8,128]{2,1,0:T(8,128)S(1)} %get-tuple-element.14), kind=kOutput, calls=%fused_computation.17 | convolution fusion | flops 405798912 | bytes 8798208 | tf_op jit(solution)/shard_map/ycmq,qyb->mycb/dot_general | solution.py:87
  86.9 2.9 %copy.39 = f32[128,4096]{1,0:T(8,128)} copy(f32[128,4096]{0,1:T(8,128)} %bitcast.81) | data formatting | bytes 4194304 | tf_op jit(solution)/shard_map/reshape | solution.py:93
  89.9 6.0 %collective-permute-done.4 = bf16[256,2,512]{2,0,1:T(8,128)(2,1)S(1)} collective-permute-done((bf16[256,2,512]{2,0,1:T(8,128)(2,1)}, bf16[256,2,512]{2,0,1:T(8,128)(2,1)S(1)}, u32[]{:S(2)}, u32[]{:S(2)}) %collective-permute-start.4) | collective-permute-done | bytes 524320 | tf_op jit(solution)/shard_map/ppermute | solution.py:16
  95.9 2.1 %pad_maximum_fusion.1 = (bf16[512,1,512]{2,0,1:T(8,128)(2,1)}, bf16[512,1,512]{2,0,1:T(8,128)(2,1)}) fusion(bf16[256,2,512]{2,0,1:T(8,128)(2,1)} %convolution_convert_fusion, bf16[256,2,512]{2,0,1:T(8,128)(2,1)S(1)} %collective-permute-done.4), kind=kLoop, calls=%fused_computation.40 | loop fusion | flops 2097152 | bytes 2097152 | tf_op jit(solution)/shard_map/concatenate | solution.py:94
  97.9 1.2 reshape_squeeze.27
  99.1 4.5 %fusion.15 = f32[4,512,128,8]{2,1,3,0:T(8,128)} fusion(bf16[128,4,8,128]{3,2,1,0:T(8,128)(2,1)S(1)} %bitcast.78, bf16[512,4,128,1]{2,1,0,3:T(4,128)(2,1)S(1)} %bitcast.79), kind=kOutput, calls=%fused_computation.32 | convolution fusion | flops 536870912 | bytes 9961472 | tf_op jit(solution)/shard_map/tgrd,kgd->grtk/dot_general | solution.py:20
  103.6 1.3 copy.49
  104.9 8.9 %fusion.39 = (f32[4,8,128]{2,1,0:T(8,128)S(1)}, f32[4,8,128,512]{2,3,1,0:T(8,128)S(1)}) fusion(f32[4,512,128,8]{2,1,3,0:T(8,128)} %fusion.15, pred[128,512]{0,1:T(8,128)(4,1)S(1)} %compare_and_fusion), kind=kOutput, calls=%fused_computation.71 | output fusion | flops 12583423 | bytes 16859136 | tf_op jit(solution)/shard_map/sub | solution.py:24
  113.8 2.3 %fusion.8 = f32[4,128,8,128]{3,1,2,0:T(8,128)} fusion(bf16[512,4,128,1]{0,2,3,1:T(8,128)(2,1)S(1)} %bitcast.84, f32[4,8,128,512]{2,3,1,0:T(8,128)S(1)} %get-tuple-element.19, f32[128]{0:T(128)S(1)} %compare_convert_fusion, f32[4,8,128]{2,1,0:T(8,128)S(1)} %get-tuple-element.18), kind=kOutput, calls=%fused_computation.14 | convolution fusion | flops 543162368 | bytes 11026944 | tf_op jit(solution)/shard_map/ycmq,qyb->mycb/dot_general | solution.py:107
  116.1 2.9 %copy.38 = f32[128,4096]{1,0:T(8,128)} copy(f32[128,4096]{0,1:T(8,128)} %bitcast.80) | data formatting | bytes 4194304 | tf_op jit(solution)/shard_map/reshape | solution.py:113
  119.0 3.5 %add_convert_fusion = bf16[128,4096]{1,0:T(8,128)(2,1)} fusion(f32[128,4096]{1,0:T(8,128)} %copy.39, f32[128,4096]{1,0:T(8,128)} %copy.38, f32[4096]{0:T(1024)S(1)} %broadcast_bitcast_fusion), kind=kLoop, calls=%fused_computation.19 | loop fusion | flops 1572864 | bytes 5259264 | tf_op jit(solution)/shard_map/convert_element_type | solution.py:115
  (38 shorter events, 1.2 us)
Async XLA Ops:
  7.4 6.0 %copy-start = (bf16[640,1280]{1,0:T(8,128)(2,1)S(1)}, bf16[640,1280]{1,0:T(8,128)(2,1)}, u32[]{:S(2)}) copy-start(bf16[640,1280]{1,0:T(8,128)(2,1)} %param.15) | copy-start | bytes 4915204
  7.4 44.7 %all-reduce.2.cloned.1.call-start = ((), (), s32[]{:S(2)}) async-start(), calls=%async_computation | async-start | bytes 2621440 | tf_op jit(solution)/shard_map/psum | solution.py:56
  13.4 1.9 %copy-start.3 = (bf16[160,2,512]{2,1,0:T(2,128)(2,1)S(1)}, bf16[160,2,512]{2,1,0:T(2,128)(2,1)}, u32[]{:S(2)}) copy-start(bf16[160,2,512]{2,1,0:T(2,128)(2,1)} %param.16) | copy-start | bytes 983044
  13.4 2.7 %copy-start.5 = (s32[128]{0:T(128)S(1)}, s32[128]{0:T(128)}, u32[]{:S(2)}) copy-start(s32[128]{0:T(128)} %param.11) | copy-start | bytes 1540
  13.4 6.1 %copy-start.4 = (bf16[2,128,512]{2,1,0:T(8,128)(2,1)S(1)}, bf16[2,128,512]{2,1,0:T(8,128)(2,1)}, u32[]{:S(2)}) copy-start(bf16[2,128,512]{2,1,0:T(8,128)(2,1)} %param.10) | copy-start | bytes 786436
  13.4 8.2 %copy-start.7 = (f32[32]{0:T(128)S(1)}, f32[32]{0:T(128)}, u32[]{:S(2)}) copy-start(f32[32]{0:T(128)} %param.17) | copy-start | bytes 388
  13.4 8.2 %copy-start.6 = (s32[128,2]{0,1:T(2,128)S(1)}, s32[128,2]{0,1:T(2,128)}, u32[]{:S(2)}) copy-start(s32[128,2]{0,1:T(2,128)} %param.12) | copy-start | bytes 3076
  15.2 60.3 %all-gather.2.cloned.1.call-start = ((), (), s32[]{:S(2)}) async-start(), calls=%async_computation.1 | async-start | bytes 2949120 | tf_op jit(solution)/shard_map/all_gather | solution.py:63
  16.1 6.3 %collective-permute-start.2 = (s32[128]{0:T(128)S(1)}, s32[128]{0:T(128)S(1)}, u32[]{:S(2)}, u32[]{:S(2)}) collective-permute-start(s32[128]{0:T(128)S(1)} %copy-done.5), channel_id=1, source_target_pairs={{0,2},{2,4},{4,6},{6,8},{8,10},{10,12},{12,14},{1,3},{3,5},{5,7},{... | collective-permute-start | bytes 1544 | tf_op jit(solution)/shard_map/ppermute | solution.py:16
  19.7 12.5 %collective-permute-start = (bf16[2,128,512]{1,2,0:T(8,128)(2,1)S(1)}, bf16[2,128,512]{1,2,0:T(8,128)(2,1)S(1)}, u32[]{:S(2)}, u32[]{:S(2)}) collective-permute-start(bf16[2,128,512]{1,2,0:T(8,128)(2,1)S(1)} %copy.24), channel_id=1, source_target_pairs={{0,2},{2,4},{4,6},{6,8},{8,10},{10,12},{12,14},{1,3},{3,5},{5,7},{... | collective-permute-start | bytes 786440 | tf_op jit(solution)/shard_map/ppermute | solution.py:16
  22.4 11.6 %collective-permute-start.3 = (s32[128]{0:T(128)S(1)}, s32[128]{0:T(128)S(1)}, u32[]{:S(2)}, u32[]{:S(2)}) collective-permute-start(s32[128]{0:T(128)S(1)} %collective-permute-done.2), channel_id=1, source_target_pairs={{0,2},{2,4},{4,6},{6,8},{8,10},{10,12},{12,14},{1,3},{3,5},{5,7},{... | collective-permute-start | bytes 1544 | tf_op jit(solution)/shard_map/ppermute | solution.py:16
  32.1 14.3 %collective-permute-start.1 = (bf16[2,128,512]{1,2,0:T(8,128)(2,1)S(1)}, bf16[2,128,512]{1,2,0:T(8,128)(2,1)S(1)}, u32[]{:S(2)}, u32[]{:S(2)}) collective-permute-start(bf16[2,128,512]{1,2,0:T(8,128)(2,1)S(1)} %collective-permute-done), channel_id=1, source_target_pairs={{0,2},{2,4},{4,6},{6,8},{8,10},{10,12},{12,14},{1,3},{3,5},{5,7},{... | collective-permute-start | bytes 786440 | tf_op jit(solution)/shard_map/ppermute | solution.py:16
  48.4 3.7 %copy-start.1 = (bf16[256,1280]{1,0:T(8,128)(2,1)S(1)}, bf16[256,1280]{1,0:T(8,128)(2,1)}, u32[]{:S(2)}) copy-start(bf16[256,1280]{1,0:T(8,128)(2,1)} %param.13) | copy-start | bytes 1966084
  75.5 6.5 %copy-start.2 = (bf16[1,384,512]{1,2,0:T(8,128)(2,1)S(1)}, bf16[1,384,512]{1,2,0:T(8,128)(2,1)}, u32[]{:S(2)}) copy-start(bf16[1,384,512]{1,2,0:T(8,128)(2,1)} %get-tuple-element.11) | copy-start | bytes 1179652
  79.4 16.5 %collective-permute-start.4 = (bf16[256,2,512]{2,0,1:T(8,128)(2,1)}, bf16[256,2,512]{2,0,1:T(8,128)(2,1)S(1)}, u32[]{:S(2)}, u32[]{:S(2)}) collective-permute-start(bf16[256,2,512]{2,0,1:T(8,128)(2,1)} %convolution_convert_fusion), channel_id=1, source_target_pairs={{0,2},{2,4},{4,6},{6,8},{8,10},{10,12},{12,14},{1,3},{3,5},{5,7},{... | collective-permute-start | bytes 1572872 | tf_op jit(solution)/shard_map/ppermute | solution.py:16
Sparse Core Ops, SparseCore 0:
  15.4 21.2 all-reduce.1
Sparse Core Ops, SparseCore 1:
  17.9 57.5 all-gather.1
where the time goes:
time: 131 us; the launch traced here: 130 us
  waiting for transfers between devices  46.2 us (35%)
  matrix products  22.5 us (17%)
  other arithmetic  20.2 us (15%)
  between operations  15.1 us (12%)
  local copies, waits for them, and re-layouts  13.5 us (10%)
  starting transfers between devices  12.4 us (9%)
    ppermute x5, waiting for transfers between devices, passed_along(): return lax.ppermute(block, axis, route)  24.3 us
    all_gather x1, waiting for transfers between devices, per_device(): lax.all_gather(cross_keyvalue_weight, 'seq', axis=0, tiled=True)  21.8 us
    sub x2, other arithmetic, attend_heads(): return jax.nn.softmax(scores, axis=-1)  12.6 us
    ppermute x5, starting transfers between devices, passed_along(): return lax.ppermute(block, axis, route)  12.3 us
    dot_general x2, matrix products, attend_heads(): jnp.einsum('tgrd,kgd->grtk', query_rows, keys, preferred_element_type=jnp...  5.54 us
    dot_general x1, matrix products, per_device(): jnp.einsum('ycmq,qyb->mycb', self_attention_weights, all_keyval[1].reshap...  4.89 us
    dot_general x1, matrix products, per_device(): jnp.einsum('ic,cjf->ijf', image_norm, lax.all_gather(cross_keyvalue_weigh...  3.87 us
    convert_element_type x1, other arithmetic, per_device(): (self_output + gate_cols[None, :] * cross_output).astype(jnp.bfloat16)  3.46 us
  transfers between devices with their start and end apart: 7, of which 5 were waited for; matrix products, arithmetic and copies ran while one was open for 14% of the time, Pallas kernels for 0%

commit v1 on v0

v1 whole, which is shorter than its diff:
```python
import functools
import math

import jax
import jax.numpy as jnp
from jax import lax
from jax.experimental import pallas as pl
from jax.experimental.pallas import tpu as pltpu
from jax.sharding import PartitionSpec as P

HEAD_SIZE = 128
VHD = 80
MESH = pl.DeviceIdType.MESH
BIG = -1e30
LOG2E = math.log2(math.e)
RING_PLACES = 8
F32 = jnp.float32
BF16 = jnp.bfloat16


def dot_t(a, b):
    return lax.dot_general(a, b, (((1,), (1,)), ((), ())), preferred_element_type=F32)


def attend(q, k, v, bias):
    s = dot_t(q, k) * (LOG2E / math.sqrt(HEAD_SIZE)) + bias
    m = jnp.max(s, axis=-1, keepdims=True)
    p = jnp.exp2(s - m).astype(BF16)
    o = jnp.dot(p, jnp.concatenate([v, jnp.ones_like(v)], axis=1), preferred_element_type=F32)
    return o[:, :HEAD_SIZE] / o[:, HEAD_SIZE:]


def kernel(
    n, ring, q_hbm, tkv_hbm, doc_row, doc_col, span, hid_hbm, vqkv_hbm, wo_hbm, w_hbm, gate,
    out,
    q, tkv, docs, hid, vqkv, wo, w, va, mix, img, ikv, self_out, sems, rsems, lsems,
):
    g, s, h = lax.axis_index("groups"), lax.axis_index("seq"), lax.axis_index("head")
    rows = q.shape[0]
    tile = hid.shape[0]
    half = tile // 2
    width = hid.shape[1]
    kv_cols = tkv.shape[2]
    kv_heads = kv_cols // HEAD_SIZE
    ratio = q.shape[1] // kv_cols
    shard = w_hbm.shape[0]
    part = vqkv.shape[2]
    counter = iter(range(64))

    local = []

    def fetch(src, dst):
        c = pltpu.make_async_copy(src, dst, lsems.at[len(local)])
        c.start()
        local.append(c)
        return c

    def remote(src, dst, to):
        i = next(counter)
        return pltpu.make_async_remote_copy(
            src_ref=src, dst_ref=dst, send_sem=sems.at[i], recv_sem=rsems.at[i],
            device_id=to, device_id_type=MESH,
        )

    get_vqkv = fetch(vqkv_hbm, vqkv)
    get_wo = fetch(wo_hbm, wo.at[h])
    get_hid = fetch(hid_hbm, hid)
    my_rows = pl.ds(pl.multiple_of(s * shard, 16), shard) if ring else pl.ds(0, shard)
    get_w = fetch(w_hbm, w.at[my_rows])
    get_tkv = fetch(tkv_hbm, tkv.at[:, pl.ds(2 * rows, rows)])
    get_q = fetch(q_hbm, q)

    sibling = (g, s, 1 - h)
    barrier = pltpu.get_barrier_semaphore()

    def greet(to):
        pl.semaphore_signal(barrier, inc=1, device_id=to, device_id_type=MESH)

    greet(sibling)
    greets = 1
    if ring:
        place = jnp.where(s % 2 == 0, s // 2, RING_PLACES - 1 - s // 2)

        def at_place(r):
            r = (r + RING_PLACES) % RING_PLACES
            return jnp.where(r < RING_PLACES // 2, 2 * r, 2 * RING_PLACES - 1 - 2 * r)

        right, left = (g, at_place(place + 1), h), (g, at_place(place - 1), h)
        partner = (1 - g, s, h)
        for to in (right, left, partner):
            greet(to)
        greets = 4
    for d in (1, 2):
        @pl.when(s + d < n)
        def _():
            greet((g, jnp.minimum(s + d, n - 1), h))

        @pl.when(s - d >= 0)
        def _():
            greet((g, jnp.maximum(s - d, 0), h))
    near = sum(
        jnp.where(s + d < n, 1, 0) + jnp.where(s - d >= 0, 1, 0) for d in (1, 2)
    )
    pl.semaphore_wait(barrier, greets + near)

    if ring:
        over = shard // 16 * 2 // 5 * 16
        share = shard - over
        off = pl.multiple_of(g * over, 16)
        give = pl.multiple_of(g * share, 16)

        def piece(place_of, start, size):
            at = at_place(place_of) * shard + start
            return w.at[pl.ds(pl.multiple_of(at, 16), size)]

        own = w_hbm.at[pl.ds(off, share)]
        cw, ccw, across = [], [], []
        half_share = share // 2

    def ring_start(k):
        if not ring:
            return
        if k < 4:
            a, b = piece(place - k + 1, off, share), piece(place + k - 1, off, share)
            cw.append(remote(own if k == 1 else a, a, right))
            ccw.append(remote(own if k == 1 else b, b, left))
        else:
            a = piece(place - 3, off, half_share)
            b = piece(place + 3, off + half_share, half_share)
            cw.append(remote(a, a, right))
            ccw.append(remote(b, b, left))
        cw[-1].start()
        ccw[-1].start()

    def ring_service(k):
        if not ring:
            return
        cw[k - 1].wait_recv()
        ccw[k - 1].wait_recv()
        if k < 4:
            ring_start(k + 1)
        for at in (place - k, place + k)[: 1 if k == 4 else 2]:
            block = piece(at, give, over)
            across.append(remote(block, block, partner))
            across[-1].start()

    ring_start(1)
    send_wo = remote(wo_hbm, wo.at[h], sibling)
    send_wo.start()
    text = []
    for d in (1, 2):
        to = (g, jnp.minimum(s + d, n - 1), h)
        text.append((
            d,
            remote(tkv_hbm, tkv.at[:, pl.ds((2 - d) * rows, rows)], to),
            remote(doc_row, docs.at[2 - d], to),
        ))

        @pl.when(s + d < n)
        def _():
            text[-1][1].start()
            text[-1][2].start()

        @pl.when(s - d < 0)
        def _():
            tkv[:, (2 - d) * rows : (3 - d) * rows] = jnp.zeros((2, rows, kv_cols), BF16)
            docs[2 - d] = jnp.full((1, rows), -1, jnp.int32)

    @pl.when(s == 0)
    def _():
        img[:tile] = jnp.zeros((tile, width), BF16)

    get_vqkv.wait()
    column = lax.broadcasted_iota(jnp.int32, (tile, 256), 1)
    mix[:, :part] = jnp.zeros((tile, part), F32)
    for head in range(part // VHD):
        start = min(head * VHD // 128 * 128, part - 256)
        first = head * VHD - start
        mine = (column >= first) & (column < first + VHD)
        window = slice(start, start + 256)
        vq = jnp.where(mine, vqkv[0, :, window], jnp.zeros((), BF16))
        sc = dot_t(vq, vqkv[1, :, window]) * (LOG2E / math.sqrt(VHD))
        p = jnp.exp2(sc - jnp.max(sc, axis=-1, keepdims=True))
        p = (p * (1.0 / jnp.sum(p, axis=-1, keepdims=True))).astype(BF16)
        o = jnp.dot(p, vqkv[2, :, window], preferred_element_type=F32)
        mix[:, window] = mix[:, window] + jnp.where(mine, o, 0.0)
        if head == 3:
            ring_service(1)
    va[h] = mix[:, :part].astype(BF16)
    send_va = remote(va.at[h], va.at[h], sibling)
    send_va.start()

    get_wo.wait()
    get_hid.wait()
    mix[...] = hid[...].astype(F32) + jnp.dot(va[h], wo[h], preferred_element_type=F32)
    send_wo.wait_recv()
    send_va.wait_recv()
    mixed = mix[...] + jnp.dot(va[1 - h], wo[1 - h], preferred_element_type=F32)
    norm = mixed * lax.rsqrt(jnp.mean(mixed * mixed, axis=-1, keepdims=True) + 1e-5)
    img[tile:] = norm.astype(BF16)
    mine_prev = img.at[pl.ds(pl.multiple_of(h * half, 16), half)]
    send_img = remote(
        img.at[pl.ds(pl.multiple_of(tile + h * half, 16), half)], mine_prev,
        (g, jnp.minimum(s + 1, n - 1), h),
    )
    pass_img = remote(mine_prev, mine_prev, sibling)

    @pl.when(s + 1 < n)
    def _():
        send_img.start()

    ring_service(2)

    for d, kv_copy, doc_copy in text:
        @pl.when(s - d >= 0)
        def _():
            kv_copy.wait_recv()
            doc_copy.wait_recv()
    get_tkv.wait()
    get_q.wait()
    key_docs = jnp.concatenate([docs[0], docs[1], doc_row[...]], axis=1)
    key_at = lax.broadcasted_iota(jnp.int32, (rows, 3 * rows), 1) - 2 * rows
    query_at = lax.broadcasted_iota(jnp.int32, (rows, 3 * rows), 0)
    seen = (key_docs == doc_col[...]) & (key_at <= query_at) & (key_at + s * rows >= 0)
    bias = jnp.where(seen, 0.0, BIG)
    bias = jnp.concatenate([bias, bias], axis=0)

    def query_pair(kv_head, pair):
        at = pl.multiple_of((kv_head * ratio + 2 * pair) * HEAD_SIZE, 128)
        return at, jnp.concatenate(
            [q[:, pl.ds(at, HEAD_SIZE)], q[:, pl.ds(at + HEAD_SIZE, HEAD_SIZE)]], axis=0
        )

    def self_head(kv_head, _):
        cols = pl.ds(pl.multiple_of(kv_head * HEAD_SIZE, 128), HEAD_SIZE)
        k, v = tkv[0, :, cols], tkv[1, :, cols]
        for pair in range(ratio // 2):
            at, two = query_pair(kv_head, pair)
            o = attend(two, k, v, bias)
            self_out[:, pl.ds(at, HEAD_SIZE)] = o[:rows]
            self_out[:, pl.ds(at + HEAD_SIZE, HEAD_SIZE)] = o[rows:]
        return 0

    lax.fori_loop(0, kv_heads // 2, self_head, 0)
    ring_service(3)

    @pl.when(s >= 1)
    def _():
        send_img.wait_recv()
        pass_img.start()

    lax.fori_loop(kv_heads // 2, kv_heads, self_head, 0)
    ring_service(4)

    @pl.when(s >= 1)
    def _():
        pass_img.wait_recv()

    get_w.wait()
    if ring:
        for c in across:
            c.wait_recv()

    def project(i, _):
        cols = pl.ds(pl.multiple_of(i * 256, 256), 256)
        ikv[:, cols] = jnp.dot(img[...], w[:, cols], preferred_element_type=F32).astype(BF16)
        return 0

    lax.fori_loop(0, ikv.shape[1] // 256, project, 0)

    low, high = span[:, 0:1], span[:, 1:2]
    tile_of = s - 1 + lax.broadcasted_iota(jnp.int32, (rows, 2 * tile), 1) // tile
    seen_tiles = (tile_of >= low) & (tile_of < high)
    tile_bias = jnp.where(seen_tiles, 0.0, BIG)
    tile_bias = jnp.concatenate([tile_bias, tile_bias], axis=0)
    present = jnp.where(high > low, 1.0, 0.0)
    gates = jnp.tanh(gate[...])
    gate_at = lax.broadcasted_iota(jnp.int32, gates.shape, 1)

    def cross_head(kv_head, _):
        cols = pl.ds(pl.multiple_of(kv_head * HEAD_SIZE, 128), HEAD_SIZE)
        v_cols = pl.ds(pl.multiple_of(kv_cols + kv_head * HEAD_SIZE, 128), HEAD_SIZE)
        k, v = ikv[:, cols], ikv[:, v_cols]
        for pair in range(ratio // 2):
            at, two = query_pair(kv_head, pair)
            o = attend(two, k, v, tile_bias)
            for j in (0, 1):
                of = kv_head * ratio + 2 * pair + j
                t = jnp.sum(jnp.where(gate_at == of, gates, 0.0), axis=1, keepdims=True)
                where = pl.ds(at + j * HEAD_SIZE, HEAD_SIZE)
                total = self_out[:, where] + (t * present) * o[j * rows : (j + 1) * rows]
                out[:, where] = total.astype(BF16)
        return 0

    lax.fori_loop(0, kv_heads, cross_head, 0)

    send_wo.wait_send()
    send_va.wait_send()
    if ring:
        for c in cw + ccw + across:
            c.wait_send()
    for d, kv_copy, doc_copy in text:
        @pl.when(s + d < n)
        def _():
            kv_copy.wait_send()
            doc_copy.wait_send()

    @pl.when(s + 1 < n)
    def _():
        send_img.wait_send()

    @pl.when(s >= 1)
    def _():
        pass_img.wait_send()


def per_device(
    groups, n, text_query_rows, text_key_value, doc_ids, tile_span, vision_hidden, vision_qkv,
    vision_out_weight, cross_keyvalue_weight, cross_gate,
):
    rows, q_cols = text_query_rows.shape
    tile, width = vision_hidden.shape
    kv_cols = text_key_value.shape[2]
    part = vision_qkv.shape[2]
    shard = cross_keyvalue_weight.shape[0]
    ring = n == RING_PLACES and groups == 2 and shard % 32 == 0
    weight = cross_keyvalue_weight.reshape(shard, 2 * kv_cols)
    if not ring:
        weight = lax.all_gather(weight, "seq", axis=0, tiled=True)
    anywhere = pl.BlockSpec(memory_space=pl.ANY)
    vmem = pl.BlockSpec(memory_space=pltpu.VMEM)
    return pl.pallas_call(
        functools.partial(kernel, n, ring),
        out_shape=jax.ShapeDtypeStruct((rows, q_cols), BF16),
        in_specs=[anywhere, anywhere, vmem, vmem, vmem, anywhere, anywhere, anywhere, anywhere, vmem],
        out_specs=vmem,
        scratch_shapes=[
            pltpu.VMEM((rows, q_cols), BF16),
            pltpu.VMEM((2, 3 * rows, kv_cols), BF16),
            pltpu.VMEM((2, 1, rows), jnp.int32),
            pltpu.VMEM((tile, width), BF16),
            pltpu.VMEM((3, tile, part), BF16),
            pltpu.VMEM((2, part, width), BF16),
            pltpu.VMEM((width, 2 * kv_cols), BF16),
            pltpu.VMEM((2, tile, part), BF16),
            pltpu.VMEM((tile, width), F32),
            pltpu.VMEM((2 * tile, width), BF16),
            pltpu.VMEM((2 * tile, 2 * kv_cols), BF16),
            pltpu.VMEM((rows, q_cols), F32),
            pltpu.SemaphoreType.DMA((32,)),
            pltpu.SemaphoreType.DMA((32,)),
            pltpu.SemaphoreType.DMA((8,)),
        ],
        compiler_params=pltpu.CompilerParams(
            collective_id=0, has_side_effects=True, vmem_limit_bytes=48 * 1024 * 1024
        ),
    )(
        text_query_rows, text_key_value, doc_ids.reshape(1, rows), doc_ids.reshape(rows, 1),
        tile_span, vision_hidden, vision_qkv, vision_out_weight, weight,
        cross_gate.reshape(1, -1),
    )


def solution(mesh):
    placed = (
        P(("groups", "seq"), "head"),
        P(None, ("groups", "seq"), "head"),
        P(("groups", "seq")),
        P(("groups", "seq"), None),
        P(("groups", "seq"), None),
        P(None, ("groups", "seq"), "head"),
        P("head", None),
        P("seq", None, "head"),
        P("head"),
    )
    return jax.shard_map(
        functools.partial(per_device, mesh.shape["groups"], mesh.shape["seq"]),
        mesh=mesh,
        in_specs=placed,
        out_specs=P(("groups", "seq"), "head"),
        check_vma=False,
    )
```

time: 131 us -> 63.4 us (0.48)
  Pallas kernels: 0 us -> 52.3 us
  waiting for transfers between devices: 46.2 us -> 0 us
  matrix products: 22.5 us -> 0 us
  other arithmetic: 20.2 us -> 0 us
  between operations: 15.1 us -> 0.03 us
  starting transfers between devices: 12.4 us -> 0 us
  local copies, waits for them, and re-layouts: 13.5 us -> 10.7 us
    pallas_call x0 -> x1, Pallas kernels: none -> 52.3 us  [per_device(): pl.pallas_call(functools.partial(kernel, n, ring), out_shape=jax.ShapeDty...]
    ppermute x5 -> x0, waiting for transfers between devices: 24.3 us -> none  [passed_along(): return lax.ppermute(block, axis, route)]
    all_gather x1 -> x0, waiting for transfers between devices: 21.8 us -> none  [per_device(): lax.all_gather(cross_keyvalue_weight, 'seq', axis=0, tiled=True)]
    dot_general x7 -> x0, matrix products: 20.3 us -> none  [the longest x2 5.54 us: attend_heads(): jnp.einsum('tgrd,kgd->grtk', query_rows, keys, preferred_element_type=jnp...]
    sub x2 -> x0, other arithmetic: 12.6 us -> none  [attend_heads(): return jax.nn.softmax(scores, axis=-1)]
    ppermute x5 -> x0, starting transfers between devices: 12.3 us -> none  [passed_along(): return lax.ppermute(block, axis, route)]
    unnamed x19 -> x17, local copies, waits for them, and re-layouts: 2.44 us -> 9.96 us
    reshape x2 -> x1, local copies, waits for them, and re-layouts: 5.86 us -> 0.76 us  [per_device(): doc_ids.reshape(rows, 1)]
  transfers between devices with their start and end apart: 7 -> 0, of which waited for: 5 -> 0; matrix products, arithmetic and copies ran while one was open for 14% -> 0% of each run, Pallas kernels for 0% -> 0%
where the time goes in v1:
time: 63.4 us; the launch traced here: 63 us
  Pallas kernels  52.3 us (82%)
  local copies, waits for them, and re-layouts  10.7 us (17%)
    pallas_call x1, Pallas kernels, per_device(): pl.pallas_call(functools.partial(kernel, n, ring), out_shape=jax.ShapeDty...  52.3 us
    unnamed x17, local copies, waits for them, and re-layouts  9.96 us

profile of v1, /device:TPU:24, one launch (start us, length us, event | category | flops | bytes accessed | tf_op | source)
XLA Modules:
  0.0 63.0 jit_solution(12063617198689948487)
XLA Ops:
  0.0 0.8 %copy.11.span = s32[128,2]{1,0:T(8,128)S(1)} copy(s32[128,2]{0,1:T(2,128)} %param.12) | data formatting | bytes 2048 | tf_op args[3]
  0.8 0.8 %copy.10.doc_col = s32[128,1]{1,0:T(8,128)S(1)} copy(s32[128,1]{0,1:T(1,128)} %bitcast.6) | data formatting | bytes 1024 | tf_op jit(solution)/shard_map/reshape | solution.py:358
  1.5 1.0 %copy.12 = bf16[20,8,2,512]{3,1,2,0:T(8,128)(2,1)S(1)} copy(bf16[20,8,2,512]{3,2,1,0:T(2,128)(2,1)} %bitcast.9) | data formatting | bytes 655360
  2.6 0.0 copy-start
  2.6 1.4 %copy-done = bf16[640,1280]{1,0:T(8,128)(2,1)S(1)} copy-done((bf16[640,1280]{1,0:T(8,128)(2,1)S(1)}, bf16[640,1280]{1,0:T(8,128)(2,1)}, u32[]{:S(2)}) %copy-start) | copy-done | bytes 1638424
  4.0 0.0 copy-start.1
  4.0 1.2 %copy-done.1 = bf16[128,4096]{1,0:T(8,128)(2,1)S(1)} copy-done((bf16[128,4096]{1,0:T(8,128)(2,1)S(1)}, bf16[128,4096]{1,0:T(8,128)(2,1)}, u32[]{:S(2)}) %copy-start.1) | copy-done | bytes 1048600
  5.2 0.0 copy-start.2
  5.2 1.2 %copy-done.2 = bf16[3,256,640]{2,1,0:T(8,128)(2,1)S(1)} copy-done((bf16[3,256,640]{2,1,0:T(8,128)(2,1)S(1)}, bf16[3,256,640]{2,1,0:T(8,128)(2,1)}, u32[]{:S(2)}) %copy-start.2) | copy-done | bytes 983064
  6.4 0.0 copy-start.3
  6.4 1.1 %copy-done.3 = bf16[256,1280]{1,0:T(8,128)(2,1)S(1)} copy-done((bf16[256,1280]{1,0:T(8,128)(2,1)S(1)}, bf16[256,1280]{1,0:T(8,128)(2,1)}, u32[]{:S(2)}) %copy-start.3) | copy-done | bytes 655384
  7.5 0.0 copy-start.4
  7.5 0.9 %copy-done.4 = bf16[2,128,512]{2,1,0:T(8,128)(2,1)S(1)} copy-done((bf16[2,128,512]{2,1,0:T(8,128)(2,1)S(1)}, bf16[2,128,512]{2,1,0:T(8,128)(2,1)}, u32[]{:S(2)}) %copy-start.4) | copy-done | bytes 262168
  8.5 0.0 copy-start.5
  8.5 0.7 %copy-done.5 = s32[128]{0:T(128)S(1)} copy-done((s32[128]{0:T(128)S(1)}, s32[128]{0:T(128)}, u32[]{:S(2)}) %copy-start.5) | copy-done | bytes 536
  9.1 0.0 copy-start.6
  9.1 0.7 %copy-done.6 = f32[32]{0:T(128)S(1)} copy-done((f32[32]{0:T(128)S(1)}, f32[32]{0:T(128)}, u32[]{:S(2)}) %copy-start.6) | copy-done | bytes 152
  9.8 52.3 %shard_map.91 = bf16[128,4096]{1,0:T(8,128)(2,1)S(1)} custom-call(bf16[128,4096]{1,0:T(8,128)(2,1)S(1)} %copy-done.1, bf16[2,128,512]{2,1,0:T(8,128)(2,1)S(1)} %copy-done.4, s32[1,128]{1,0:T(1,128)S(1)} %bitcast.7, s32[128,1]{1,0:T(8,128)S(1)} %copy.10.doc_col, s32[128,2]{1,0:T(8,128)S(1)} %copy.11.span, bf16[256,1280]{1,0:T(8,128)(2,1)S(1)} %copy-done.3, ...), custom_call_target="tpu_custom_call" | custom-call | tf_op jit(solution)/shard_map/pallas_call | solution.py:332
  62.1 1.0 %copy.14 = bf16[128,4096]{1,0:T(8,128)(2,1)} copy(bf16[128,4096]{1,0:T(8,128)(2,1)S(1)} %shard_map.91) | data formatting | bytes 2097152
Async XLA Ops:
  2.6 1.4 %copy-start = (bf16[640,1280]{1,0:T(8,128)(2,1)S(1)}, bf16[640,1280]{1,0:T(8,128)(2,1)}, u32[]{:S(2)}) copy-start(bf16[640,1280]{1,0:T(8,128)(2,1)} %wo_hbm.1) | copy-start | bytes 4915204
  4.0 1.2 %copy-start.1 = (bf16[128,4096]{1,0:T(8,128)(2,1)S(1)}, bf16[128,4096]{1,0:T(8,128)(2,1)}, u32[]{:S(2)}) copy-start(bf16[128,4096]{1,0:T(8,128)(2,1)} %q_hbm.1) | copy-start | bytes 3145732
  5.2 1.2 %copy-start.2 = (bf16[3,256,640]{2,1,0:T(8,128)(2,1)S(1)}, bf16[3,256,640]{2,1,0:T(8,128)(2,1)}, u32[]{:S(2)}) copy-start(bf16[3,256,640]{2,1,0:T(8,128)(2,1)} %vqkv_hbm.1) | copy-start | bytes 2949124
  6.4 1.1 %copy-start.3 = (bf16[256,1280]{1,0:T(8,128)(2,1)S(1)}, bf16[256,1280]{1,0:T(8,128)(2,1)}, u32[]{:S(2)}) copy-start(bf16[256,1280]{1,0:T(8,128)(2,1)} %hid_hbm.1) | copy-start | bytes 1966084
  7.5 0.9 %copy-start.4 = (bf16[2,128,512]{2,1,0:T(8,128)(2,1)S(1)}, bf16[2,128,512]{2,1,0:T(8,128)(2,1)}, u32[]{:S(2)}) copy-start(bf16[2,128,512]{2,1,0:T(8,128)(2,1)} %tkv_hbm.1) | copy-start | bytes 786436
  8.5 0.7 %copy-start.5 = (s32[128]{0:T(128)S(1)}, s32[128]{0:T(128)}, u32[]{:S(2)}) copy-start(s32[128]{0:T(128)} %param.11) | copy-start | bytes 1540
  9.1 0.7 %copy-start.6 = (f32[32]{0:T(128)S(1)}, f32[32]{0:T(128)}, u32[]{:S(2)}) copy-start(f32[32]{0:T(128)} %param.17) | copy-start | bytes 388

commit v2 on v1

--- a/solution.py
+++ b/solution.py
@@ -14,12 +14,20 @@
 BIG = -1e30
 LOG2E = math.log2(math.e)
 RING_PLACES = 8
+SEMS = 56
+SUBS = 2
+OVER = 4
 F32 = jnp.float32
 BF16 = jnp.bfloat16
 
 
 def dot_t(a, b):
     return lax.dot_general(a, b, (((1,), (1,)), ((), ())), preferred_element_type=F32)
+
+
+def as_column(row):
+    square = jnp.broadcast_to(row, (row.shape[1], row.shape[1]))
+    return jnp.transpose(square)[:, 0:1]
 
 
 def attend(q, k, v, bias):
@@ -31,7 +39,7 @@
 
 
 def kernel(
-    n, ring, q_hbm, tkv_hbm, doc_row, doc_col, span, hid_hbm, vqkv_hbm, wo_hbm, w_hbm, gate,
+    n, ring, q_hbm, tkv_hbm, doc_row, span, hid_hbm, vqkv_hbm, wo_hbm, w_hbm, gate,
     out,
     q, tkv, docs, hid, vqkv, wo, w, va, mix, img, ikv, self_out, sems, rsems, lsems,
 ):
@@ -45,7 +53,7 @@
     ratio = q.shape[1] // kv_cols
     shard = w_hbm.shape[0]
     part = vqkv.shape[2]
-    counter = iter(range(64))
+    counter = iter(range(SEMS))
 
     local = []
 
@@ -104,7 +112,7 @@
     pl.semaphore_wait(barrier, greets + near)
 
     if ring:
-        over = shard // 16 * 2 // 5 * 16
+        over = shard // 16 * OVER // 10 * 16
         share = shard - over
         off = pl.multiple_of(g * over, 16)
         give = pl.multiple_of(g * share, 16)
@@ -113,38 +121,34 @@
             at = at_place(place_of) * shard + start
             return w.at[pl.ds(pl.multiple_of(at, 16), size)]
 
-        own = w_hbm.at[pl.ds(off, share)]
-        cw, ccw, across = [], [], []
-        half_share = share // 2
-
-    def ring_start(k):
-        if not ring:
-            return
-        if k < 4:
-            a, b = piece(place - k + 1, off, share), piece(place + k - 1, off, share)
-            cw.append(remote(own if k == 1 else a, a, right))
-            ccw.append(remote(own if k == 1 else b, b, left))
-        else:
-            a = piece(place - 3, off, half_share)
-            b = piece(place + 3, off + half_share, half_share)
-            cw.append(remote(a, a, right))
-            ccw.append(remote(b, b, left))
-        cw[-1].start()
-        ccw[-1].start()
+        size = share // SUBS
+        right_way, left_way, across = {}, {}, []
+
+    def ring_start(k, i):
+        for way, to, back, turn in ((right_way, right, 1 - k, 0), (left_way, left, k - 1, 1)):
+            if k < 4 or i % 2 == turn:
+                dst = piece(place + back, off + i * size, size)
+                src = w_hbm.at[pl.ds(pl.multiple_of(off + i * size, 16), size)] if k == 1 else dst
+                way[k, i] = remote(src, dst, to)
+                way[k, i].start()
 
     def ring_service(k):
         if not ring:
             return
-        cw[k - 1].wait_recv()
-        ccw[k - 1].wait_recv()
-        if k < 4:
-            ring_start(k + 1)
+        for i in range(SUBS):
+            for way in (right_way, left_way):
+                if (k, i) in way:
+                    way[k, i].wait_recv()
+            if k < 4:
+                ring_start(k + 1, i)
         for at in (place - k, place + k)[: 1 if k == 4 else 2]:
             block = piece(at, give, over)
             across.append(remote(block, block, partner))
             across[-1].start()
 
-    ring_start(1)
+    if ring:
+        for i in range(SUBS):
+            ring_start(1, i)
     send_wo = remote(wo_hbm, wo.at[h], sibling)
     send_wo.start()
     text = []
@@ -221,7 +225,7 @@
     key_docs = jnp.concatenate([docs[0], docs[1], doc_row[...]], axis=1)
     key_at = lax.broadcasted_iota(jnp.int32, (rows, 3 * rows), 1) - 2 * rows
     query_at = lax.broadcasted_iota(jnp.int32, (rows, 3 * rows), 0)
-    seen = (key_docs == doc_col[...]) & (key_at <= query_at) & (key_at + s * rows >= 0)
+    seen = (key_docs == as_column(doc_row[...])) & (key_at <= query_at) & (key_at + s * rows >= 0)
     bias = jnp.where(seen, 0.0, BIG)
     bias = jnp.concatenate([bias, bias], axis=0)
 
@@ -268,7 +272,7 @@
 
     lax.fori_loop(0, ikv.shape[1] // 256, project, 0)
 
-    low, high = span[:, 0:1], span[:, 1:2]
+    low, high = as_column(span[0:1, :]), as_column(span[1:2, :])
     tile_of = s - 1 + lax.broadcasted_iota(jnp.int32, (rows, 2 * tile), 1) // tile
     seen_tiles = (tile_of >= low) & (tile_of < high)
     tile_bias = jnp.where(seen_tiles, 0.0, BIG)
@@ -297,7 +301,7 @@
     send_wo.wait_send()
     send_va.wait_send()
     if ring:
-        for c in cw + ccw + across:
+        for c in [*right_way.values(), *left_way.values(), *across]:
             c.wait_send()
     for d, kv_copy, doc_copy in text:
         @pl.when(s + d < n)
@@ -323,7 +327,7 @@
     kv_cols = text_key_value.shape[2]
     part = vision_qkv.shape[2]
     shard = cross_keyvalue_weight.shape[0]
-    ring = n == RING_PLACES and groups == 2 and shard % 32 == 0
+    ring = n == RING_PLACES and groups == 2 and shard % 160 == 0
     weight = cross_keyvalue_weight.reshape(shard, 2 * kv_cols)
     if not ring:
         weight = lax.all_gather(weight, "seq", axis=0, tiled=True)
@@ -332,7 +336,7 @@
     return pl.pallas_call(
         functools.partial(kernel, n, ring),
         out_shape=jax.ShapeDtypeStruct((rows, q_cols), BF16),
-        in_specs=[anywhere, anywhere, vmem, vmem, vmem, anywhere, anywhere, anywhere, anywhere, vmem],
+        in_specs=[anywhere, anywhere, vmem, vmem, anywhere, anywhere, anywhere, anywhere, vmem],
         out_specs=vmem,
         scratch_shapes=[
             pltpu.VMEM((rows, q_cols), BF16),
@@ -347,16 +351,16 @@
             pltpu.VMEM((2 * tile, width), BF16),
             pltpu.VMEM((2 * tile, 2 * kv_cols), BF16),
             pltpu.VMEM((rows, q_cols), F32),
-            pltpu.SemaphoreType.DMA((32,)),
-            pltpu.SemaphoreType.DMA((32,)),
+            pltpu.SemaphoreType.DMA((SEMS,)),
+            pltpu.SemaphoreType.DMA((SEMS,)),
             pltpu.SemaphoreType.DMA((8,)),
         ],
         compiler_params=pltpu.CompilerParams(
-            collective_id=0, has_side_effects=True, vmem_limit_bytes=48 * 1024 * 1024
+            collective_id=0, has_side_effects=True, vmem_limit_bytes=62 * 1024 * 1024
         ),
     )(
-        text_query_rows, text_key_value, doc_ids.reshape(1, rows), doc_ids.reshape(rows, 1),
-        tile_span, vision_hidden, vision_qkv, vision_out_weight, weight,
+        text_query_rows, text_key_value, doc_ids.reshape(1, rows), tile_span.T,
+        vision_hidden, vision_qkv, vision_out_weight, weight,
         cross_gate.reshape(1, -1),
     )
 

time: 63.4 us -> 56.9 us (0.90)
  local copies, waits for them, and re-layouts: 10.7 us -> 4.02 us
    unnamed x17 -> x2, local copies, waits for them, and re-layouts: 9.96 us -> 4.02 us
    reshape x1 -> x0, local copies, waits for them, and re-layouts: 0.76 us -> none  [per_device(): doc_ids.reshape(rows, 1)]
where the time goes in v2:
time: 56.9 us; the launch traced here: 55.9 us
  Pallas kernels  51.9 us (91%)
  local copies, waits for them, and re-layouts  4.02 us (7%)
    pallas_call x1, Pallas kernels, per_device(): pl.pallas_call(functools.partial(kernel, n, ring), out_shape=jax.ShapeDty...  51.9 us
    unnamed x2, local copies, waits for them, and re-layouts  4.02 us

profile of v2, /device:TPU:24, one launch (start us, length us, event | category | flops | bytes accessed | tf_op | source)
XLA Modules:
  0.0 55.9 jit_solution(16367192498511109029)
XLA Ops:
  0.0 1.7 %copy.10 = bf16[20,8,2,512]{3,1,2,0:T(8,128)(2,1)} copy(bf16[20,8,2,512]{3,2,1,0:T(2,128)(2,1)} %bitcast.6) | data formatting | bytes 655360
  1.7 51.9 %shard_map.91 = bf16[128,4096]{1,0:T(8,128)(2,1)} custom-call(bf16[128,4096]{1,0:T(8,128)(2,1)} %q_hbm.1, bf16[2,128,512]{2,1,0:T(8,128)(2,1)} %tkv_hbm.1, s32[1,128]{1,0:T(1,128)} %bitcast.8, s32[2,128]{1,0:T(2,128)} %bitcast.7, bf16[256,1280]{1,0:T(8,128)(2,1)} %hid_hbm.1, bf16[3,256,640]{2,1,0:T(8,128)(2,1)} %vqkv_hbm.1, bf16[640,1280]{1,0:T(8,128)(2,1)} %wo_hbm.1, ...), custom_call_target="tpu_custom_call" | custom-call | tf_op jit(solution)/shard_map/pallas_call | solution.py:336
  53.6 2.3 %copy.12 = bf16[128,4096]{1,0:T(8,128)(2,1)} copy(bf16[128,4096]{1,0:T(8,128)(2,1)} %shard_map.91) | data formatting | bytes 2097152

commit v3 on v2

--- a/solution.py
+++ b/solution.py
@@ -15,8 +15,8 @@
 LOG2E = math.log2(math.e)
 RING_PLACES = 8
 SEMS = 56
-SUBS = 2
-OVER = 4
+SUBS = 5
+OVER = 5
 F32 = jnp.float32
 BF16 = jnp.bfloat16
 
@@ -151,19 +151,32 @@
             ring_start(1, i)
     send_wo = remote(wo_hbm, wo.at[h], sibling)
     send_wo.start()
-    text = []
+    far = remote(tkv_hbm, tkv.at[:, pl.ds(0, rows)], (g, jnp.minimum(s + 2, n - 1), h))
+    odd = s % 2
+    turned = n % 2 == 0
+    step = 1 - 2 * odd
+    near_to = jnp.clip(s + step, 0, n - 1) if turned else jnp.minimum(s + 1, n - 1)
+    middle = tkv.at[:, pl.ds(rows, rows)]
+    close = remote(tkv_hbm, middle, (g, near_to, h))
+    back = remote(tkv.at[:, pl.ds(0, rows)], middle, (g, near_to, h))
+    ids = [
+        remote(doc_row, docs.at[2 - d], (g, jnp.minimum(s + d, n - 1), h)) for d in (1, 2)
+    ]
+    has_close = odd == 0 if turned else s + 1 < n
+    has_back = (odd == 1) & (s >= 2) if turned else s < 0
+
+    @pl.when(s + 2 < n)
+    def _():
+        far.start()
+
+    @pl.when(has_close)
+    def _():
+        close.start()
+
     for d in (1, 2):
-        to = (g, jnp.minimum(s + d, n - 1), h)
-        text.append((
-            d,
-            remote(tkv_hbm, tkv.at[:, pl.ds((2 - d) * rows, rows)], to),
-            remote(doc_row, docs.at[2 - d], to),
-        ))
-
         @pl.when(s + d < n)
         def _():
-            text[-1][1].start()
-            text[-1][2].start()
+            ids[d - 1].start()
 
         @pl.when(s - d < 0)
         def _():
@@ -215,11 +228,39 @@
 
     ring_service(2)
 
-    for d, kv_copy, doc_copy in text:
-        @pl.when(s - d >= 0)
-        def _():
-            kv_copy.wait_recv()
-            doc_copy.wait_recv()
+    @pl.when(s >= 2)
+    def _():
+        far.wait_recv()
+        ids[1].wait_recv()
+
+    @pl.when(has_back)
+    def _():
+        back.start()
+
+    @pl.when(s >= 1)
+    def _():
+        ids[0].wait_recv()
+
+    ring_service(3)
+    ring_service(4)
+
+    @pl.when(s >= 1)
+    def _():
+        send_img.wait_recv()
+        pass_img.start()
+
+    if turned:
+        @pl.when(odd == 1)
+        def _():
+            close.wait_recv()
+
+        @pl.when((odd == 0) & (s >= 2))
+        def _():
+            back.wait_recv()
+    else:
+        @pl.when(s >= 1)
+        def _():
+            close.wait_recv()
     get_tkv.wait()
     get_q.wait()
     key_docs = jnp.concatenate([docs[0], docs[1], doc_row[...]], axis=1)
@@ -245,16 +286,8 @@
             self_out[:, pl.ds(at + HEAD_SIZE, HEAD_SIZE)] = o[rows:]
         return 0
 
-    lax.fori_loop(0, kv_heads // 2, self_head, 0)
-    ring_service(3)
-
-    @pl.when(s >= 1)
-    def _():
-        send_img.wait_recv()
-        pass_img.start()
-
-    lax.fori_loop(kv_heads // 2, kv_heads, self_head, 0)
-    ring_service(4)
+
+    lax.fori_loop(0, kv_heads, self_head, 0)
 
     @pl.when(s >= 1)
     def _():
@@ -303,11 +336,22 @@
     if ring:
         for c in [*right_way.values(), *left_way.values(), *across]:
             c.wait_send()
-    for d, kv_copy, doc_copy in text:
+    for d in (1, 2):
         @pl.when(s + d < n)
         def _():
-            kv_copy.wait_send()
-            doc_copy.wait_send()
+            ids[d - 1].wait_send()
+
+    @pl.when(s + 2 < n)
+    def _():
+        far.wait_send()
+
+    @pl.when(has_close)
+    def _():
+        close.wait_send()
+
+    @pl.when(has_back)
+    def _():
+        back.wait_send()
 
     @pl.when(s + 1 < n)
     def _():

time: 56.9 us -> 51.3 us (0.902)
  the two profiles are of different devices: /device:TPU:24 before, /device:TPU:2 now
where the time goes in v3:
time: 51.3 us; the launch traced here: 51.1 us
  Pallas kernels  47.1 us (92%)
  local copies, waits for them, and re-layouts  4.02 us (8%)
    pallas_call x1, Pallas kernels, per_device(): pl.pallas_call(functools.partial(kernel, n, ring), out_shape=jax.ShapeDty...  47.1 us
    unnamed x2, local copies, waits for them, and re-layouts  4.02 us

profile of v3, /device:TPU:2, one launch (start us, length us, event | category | flops | bytes accessed | tf_op | source)
XLA Modules:
  0.0 51.1 jit_solution(15661009481397513661)
XLA Ops:
  0.0 1.7 %copy.10 = bf16[20,8,2,512]{3,1,2,0:T(8,128)(2,1)} copy(bf16[20,8,2,512]{3,2,1,0:T(2,128)(2,1)} %bitcast.6) | data formatting | bytes 655360
  1.7 47.1 %shard_map.91 = bf16[128,4096]{1,0:T(8,128)(2,1)} custom-call(bf16[128,4096]{1,0:T(8,128)(2,1)} %q_hbm.1, bf16[2,128,512]{2,1,0:T(8,128)(2,1)} %tkv_hbm.1, s32[1,128]{1,0:T(1,128)} %bitcast.8, s32[2,128]{1,0:T(2,128)} %bitcast.7, bf16[256,1280]{1,0:T(8,128)(2,1)} %hid_hbm.1, bf16[3,256,640]{2,1,0:T(8,128)(2,1)} %vqkv_hbm.1, bf16[640,1280]{1,0:T(8,128)(2,1)} %wo_hbm.1, ...), custom_call_target="tpu_custom_call" | custom-call | tf_op jit(solution)/shard_map/pallas_call | solution.py:380
  48.8 2.3 %copy.12 = bf16[128,4096]{1,0:T(8,128)(2,1)} copy(bf16[128,4096]{1,0:T(8,128)(2,1)} %shard_map.91) | data formatting | bytes 2097152

commit v4 on v3

--- a/solution.py
+++ b/solution.py
@@ -14,9 +14,8 @@
 BIG = -1e30
 LOG2E = math.log2(math.e)
 RING_PLACES = 8
-SEMS = 56
+SEMS = 96
 SUBS = 5
-OVER = 5
 F32 = jnp.float32
 BF16 = jnp.bfloat16
 
@@ -112,10 +111,9 @@
     pl.semaphore_wait(barrier, greets + near)
 
     if ring:
-        over = shard // 16 * OVER // 10 * 16
+        over = shard // 2
         share = shard - over
         off = pl.multiple_of(g * over, 16)
-        give = pl.multiple_of(g * share, 16)
 
         def piece(place_of, start, size):
             at = at_place(place_of) * shard + start
@@ -136,15 +134,14 @@
         if not ring:
             return
         for i in range(SUBS):
-            for way in (right_way, left_way):
+            for way, at in ((right_way, place - k), (left_way, place + k)):
                 if (k, i) in way:
                     way[k, i].wait_recv()
+                    block = piece(at, off + i * size, size)
+                    across.append(remote(block, block, partner))
+                    across[-1].start()
             if k < 4:
                 ring_start(k + 1, i)
-        for at in (place - k, place + k)[: 1 if k == 4 else 2]:
-            block = piece(at, give, over)
-            across.append(remote(block, block, partner))
-            across[-1].start()
 
     if ring:
         for i in range(SUBS):

time: 51.3 us -> 50.9 us (level)
  the two profiles are of different devices: /device:TPU:2 before, /device:TPU:24 now
where the time goes in v4:
time: 50.9 us; the launch traced here: 50.7 us
  Pallas kernels  46.7 us (92%)
  local copies, waits for them, and re-layouts  4.02 us (8%)
    pallas_call x1, Pallas kernels, per_device(): pl.pallas_call(functools.partial(kernel, n, ring), out_shape=jax.ShapeDty...  46.7 us
    unnamed x2, local copies, waits for them, and re-layouts  4.02 us

profile of v4, /device:TPU:24, one launch (start us, length us, event | category | flops | bytes accessed | tf_op | source)
XLA Modules:
  0.0 50.7 jit_solution(12919345063067859652)
XLA Ops:
  0.0 1.7 %copy.10 = bf16[20,8,2,512]{3,1,2,0:T(8,128)(2,1)} copy(bf16[20,8,2,512]{3,2,1,0:T(2,128)(2,1)} %bitcast.6) | data formatting | bytes 655360
  1.7 46.7 %shard_map.91 = bf16[128,4096]{1,0:T(8,128)(2,1)} custom-call(bf16[128,4096]{1,0:T(8,128)(2,1)} %q_hbm.1, bf16[2,128,512]{2,1,0:T(8,128)(2,1)} %tkv_hbm.1, s32[1,128]{1,0:T(1,128)} %bitcast.8, s32[2,128]{1,0:T(2,128)} %bitcast.7, bf16[256,1280]{1,0:T(8,128)(2,1)} %hid_hbm.1, bf16[3,256,640]{2,1,0:T(8,128)(2,1)} %vqkv_hbm.1, bf16[640,1280]{1,0:T(8,128)(2,1)} %wo_hbm.1, ...), custom_call_target="tpu_custom_call" | custom-call | tf_op jit(solution)/shard_map/pallas_call | solution.py:377
  48.4 2.3 %copy.12 = bf16[128,4096]{1,0:T(8,128)(2,1)} copy(bf16[128,4096]{1,0:T(8,128)(2,1)} %shard_map.91) | data formatting | bytes 2097152
